TPU v7x, 32 devices: a whole 2x2x4 slice. The times are simulated.
32 devices in a mesh: blk: 8 (over y, x, core), head: 4 (over z).
Axes of the slice: x: 2, y: 2, z: 4, core: 2. Of those that a mesh axis runs over, the one named last changes fastest.
Arguments:
- queries: bfloat16 [4096, 8192], P('blk', 'head'), may hold values from -120 to 120
- keys: bfloat16 [4096, 1024], P('blk', 'head'), may hold values from -6.5 to 6.5
- values: bfloat16 [4096, 1024], P('blk', 'head'), may hold values from -6 to 6
- w_out: bfloat16 [8192, 8192], P('head'), may hold values from -0.09375 to 0.09375
- order: int32 [16], replicated, may hold values from 0 to 15, each once
Outputs:
- mixed: bfloat16 [4096, 8192], P('blk', 'head')
Inputs may be any that keep to these rules, and one draw needn't show every extreme that they name: `order`: A permutation of 0 to 15.
All inputs are finite; a program needn't handle non-finite values.
Results may differ from a plain program's by a relative error of at most 0.015.
Values may be sent and summed in bfloat16 or wider, within the bound.
No kernel may reach another device: no remote copies, remote signals or barrier semaphores. Data moves between devices by JAX's collectives and lax.ppermute only.
A program may use at most 128 MiB of HBM per device.

v0:
```python
import math

import jax
import jax.numpy as jnp
from jax import lax
from jax.sharding import PartitionSpec as P

HD = 128


def positions(order, rows, half):
    count = order.shape[0]
    block_id = rows // half
    hit = block_id[:, None] == jnp.arange(count, dtype=jnp.int32)[None, :]
    return jnp.sum(jnp.where(hit, order[None, :], 0), axis=1) * half + rows % half


def attend(carry, k_block, v_block, key_pos, q_heads, query_pos, scale):
    top, total, summed = carry
    score = (
        jnp.einsum("kgtd,nkd->kgtn", q_heads, k_block, preferred_element_type=jnp.float32) * scale
    )
    visible = key_pos[None, None, None, :] <= query_pos[None, None, :, None]
    score = jnp.where(visible, score, -1e30)
    new_top = jnp.maximum(top, jnp.max(score, axis=-1))
    weight = jnp.where(visible, jnp.exp(score - new_top[..., None]), 0.0)
    factor = jnp.exp(top - new_top)
    total = total * factor + jnp.sum(weight, axis=-1)
    summed = summed * factor[..., None] + jnp.einsum(
        "kgtn,nkd->kgtd", weight.astype(jnp.bfloat16), v_block, preferred_element_type=jnp.float32
    )
    return (new_top, total, summed)


def per_device(queries, keys, values, w_out, order):
    tok = queries.shape[0]
    half = tok // 2
    head_size = HD
    kv_local = keys.shape[1] // head_size
    q_local = queries.shape[1] // head_size
    group = q_local // kv_local
    scale = head_size ** (-0.5)
    own = lax.axis_index("blk") * tok + jnp.arange(tok, dtype=jnp.int32)
    query_pos = positions(order, own, half)
    q_heads = jnp.transpose(queries.reshape(tok, kv_local, group, head_size), (1, 2, 0, 3))
    start_state = (
        jnp.full((kv_local, group, tok), -1e30, jnp.float32),
        jnp.zeros((kv_local, group, tok), jnp.float32),
        jnp.zeros((kv_local, group, tok, head_size), jnp.float32),
    )
    k_piece = lax.all_gather(keys, "blk", axis=0, tiled=True)
    v_piece = lax.all_gather(values, "blk", axis=0, tiled=True)
    count = k_piece.shape[0]
    width = math.gcd(count, 512)
    steps = count // width
    k_blocks = k_piece.reshape(steps, width, kv_local, head_size)
    v_blocks = v_piece.reshape(steps, width, kv_local, head_size)

    def one_block(state, inputs):
        k_block, v_block, number = inputs
        rows = number * width + jnp.arange(width, dtype=jnp.int32)
        key_pos = positions(order, rows, half)
        return (attend(state, k_block, v_block, key_pos, q_heads, query_pos, scale), None)

    result, _ = lax.scan(
        one_block, start_state, (k_blocks, v_blocks, jnp.arange(steps, dtype=jnp.int32))
    )
    top, total, summed = result
    attended = (summed / total[..., None]).astype(jnp.bfloat16)
    attended = jnp.transpose(attended, (2, 0, 1, 3)).reshape(tok, q_local * head_size)
    partial_out = jnp.dot(attended, w_out, preferred_element_type=jnp.float32)
    return lax.psum_scatter(
        partial_out.astype(jnp.bfloat16), "head", scatter_dimension=1, tiled=True
    )


def solution(mesh):
    return jax.shard_map(
        per_device,
        mesh=mesh,
        in_specs=(P("blk", "head"), P("blk", "head"), P("blk", "head"), P("head", None), P()),
        out_specs=P("blk", "head"),
        check_vma=False,
    )
```

profile of v0, /device:TPU:12, one launch (start us, length us, event | category | flops | bytes accessed | tf_op | source)
XLA Modules:
  0.0 410.0 jit_solution(4492141966524637849)
XLA Ops:
  8.1 3.9 copy.17
  12.0 3.0 copy.20
  15.2 23.0 %all-gather.3.cloned.1.call-done = bf16[4096,256]{1,0:T(8,128)(2,1)} async-done(((bf16[512,256]{1,0:T(8,128)(2,1)}), bf16[4096,256]{1,0:T(8,128)(2,1)}) %all-gather.3.cloned.1.call-update) | async-done | bytes 2097168 | tf_op jit(solution)/shard_map/all_gather | solution.py:51
  38.2 4.0 reshape.110
  42.2 25.9 %all-gather.5.cloned.1.call-done = bf16[4096,256]{1,0:T(8,128)(2,1)} async-done(((bf16[512,256]{1,0:T(8,128)(2,1)}), bf16[4096,256]{1,0:T(8,128)(2,1)}) %all-gather.5.cloned.1.call-update) | async-done | bytes 2097168 | tf_op jit(solution)/shard_map/all_gather | solution.py:52
  68.0 4.0 reshape.111
  72.0 152.9 %while.17 = (s32[]{:T(128)}, f32[2,8,512]{2,1,0:T(8,128)S(1)}, f32[2,8,512]{2,1,0:T(8,128)S(1)}, f32[2,8,512,128]{3,2,1,0:T(8,128)}, s32[8]{0:T(128)S(1)}, /*ind...) while((s32[]{:T(128)}, f32[2,8,512]{2,1,0:T(8,128)S(1)}, ...), condition=%wide.region_5.6_spmd.clone, body=%wide.region_1.5_spmd.clone.sunk | while | flops 2205497856 | bytes 63977712 | solution.py:65
  75.6 2.9 fusion.35
  78.6 4.0 fusion.36
  82.6 8.2 %fusion.38 = f32[2,8,512,128]{3,2,1,0:T(8,128)} fusion(f32[2,8,512,128]{3,2,1,0:T(8,128)} %get-tuple-element.304, f32[2,8,512]{2,1,0:T(8,128)S(1)} %get-tuple-element.286, pred[]{:T(512)S(6)} %compare.23, f32[2,512,8,512]{3,1,2,0:T(8,128)S(1)} %get-tuple-element.284, f32[2,8,512]{2,1,0:T(8,128)S(1)} %select_maximum_fusion.2, ...), kind=kOutput, calls=%fused_computation.8.clone.1 | convolution fusion | flops 1097859072 | bytes 25755648 | tf_op jit(solution)/shard_map/while/body/eval_jaxpr/kgtn,nkd->kgtd/dot_general | solution.py:29
  97.3 4.0 fusion.36
  101.3 8.6 %fusion.38 = f32[2,8,512,128]{3,2,1,0:T(8,128)} fusion(f32[2,8,512,128]{3,2,1,0:T(8,128)} %get-tuple-element.304, f32[2,8,512]{2,1,0:T(8,128)S(1)} %get-tuple-element.286, pred[]{:T(512)S(6)} %compare.23, f32[2,512,8,512]{3,1,2,0:T(8,128)S(1)} %get-tuple-element.284, f32[2,8,512]{2,1,0:T(8,128)S(1)} %select_maximum_fusion.2, ...), kind=kOutput, calls=%fused_computation.8.clone.1 | convolution fusion | flops 1097859072 | bytes 25755648 | tf_op jit(solution)/shard_map/while/body/eval_jaxpr/kgtn,nkd->kgtd/dot_general | solution.py:29
  116.5 4.0 fusion.36
  120.5 8.6 %fusion.38 = f32[2,8,512,128]{3,2,1,0:T(8,128)} fusion(f32[2,8,512,128]{3,2,1,0:T(8,128)} %get-tuple-element.304, f32[2,8,512]{2,1,0:T(8,128)S(1)} %get-tuple-element.286, pred[]{:T(512)S(6)} %compare.23, f32[2,512,8,512]{3,1,2,0:T(8,128)S(1)} %get-tuple-element.284, f32[2,8,512]{2,1,0:T(8,128)S(1)} %select_maximum_fusion.2, ...), kind=kOutput, calls=%fused_computation.8.clone.1 | convolution fusion | flops 1097859072 | bytes 25755648 | tf_op jit(solution)/shard_map/while/body/eval_jaxpr/kgtn,nkd->kgtd/dot_general | solution.py:29
  132.7 2.9 fusion.35
  135.6 4.0 fusion.36
  139.7 8.6 %fusion.38 = f32[2,8,512,128]{3,2,1,0:T(8,128)} fusion(f32[2,8,512,128]{3,2,1,0:T(8,128)} %get-tuple-element.304, f32[2,8,512]{2,1,0:T(8,128)S(1)} %get-tuple-element.286, pred[]{:T(512)S(6)} %compare.23, f32[2,512,8,512]{3,1,2,0:T(8,128)S(1)} %get-tuple-element.284, f32[2,8,512]{2,1,0:T(8,128)S(1)} %select_maximum_fusion.2, ...), kind=kOutput, calls=%fused_computation.8.clone.1 | convolution fusion | flops 1097859072 | bytes 25755648 | tf_op jit(solution)/shard_map/while/body/eval_jaxpr/kgtn,nkd->kgtd/dot_general | solution.py:29
  151.8 2.9 fusion.35
  154.8 4.0 fusion.36
  158.8 8.6 %fusion.38 = f32[2,8,512,128]{3,2,1,0:T(8,128)} fusion(f32[2,8,512,128]{3,2,1,0:T(8,128)} %get-tuple-element.304, f32[2,8,512]{2,1,0:T(8,128)S(1)} %get-tuple-element.286, pred[]{:T(512)S(6)} %compare.23, f32[2,512,8,512]{3,1,2,0:T(8,128)S(1)} %get-tuple-element.284, f32[2,8,512]{2,1,0:T(8,128)S(1)} %select_maximum_fusion.2, ...), kind=kOutput, calls=%fused_computation.8.clone.1 | convolution fusion | flops 1097859072 | bytes 25755648 | tf_op jit(solution)/shard_map/while/body/eval_jaxpr/kgtn,nkd->kgtd/dot_general | solution.py:29
  171.0 2.9 fusion.35
  173.9 4.0 fusion.36
  178.0 8.6 %fusion.38 = f32[2,8,512,128]{3,2,1,0:T(8,128)} fusion(f32[2,8,512,128]{3,2,1,0:T(8,128)} %get-tuple-element.304, f32[2,8,512]{2,1,0:T(8,128)S(1)} %get-tuple-element.286, pred[]{:T(512)S(6)} %compare.23, f32[2,512,8,512]{3,1,2,0:T(8,128)S(1)} %get-tuple-element.284, f32[2,8,512]{2,1,0:T(8,128)S(1)} %select_maximum_fusion.2, ...), kind=kOutput, calls=%fused_computation.8.clone.1 | convolution fusion | flops 1097859072 | bytes 25755648 | tf_op jit(solution)/shard_map/while/body/eval_jaxpr/kgtn,nkd->kgtd/dot_general | solution.py:29
  190.2 2.9 fusion.35
  193.1 4.0 fusion.36
  197.1 8.6 %fusion.38 = f32[2,8,512,128]{3,2,1,0:T(8,128)} fusion(f32[2,8,512,128]{3,2,1,0:T(8,128)} %get-tuple-element.304, f32[2,8,512]{2,1,0:T(8,128)S(1)} %get-tuple-element.286, pred[]{:T(512)S(6)} %compare.23, f32[2,512,8,512]{3,1,2,0:T(8,128)S(1)} %get-tuple-element.284, f32[2,8,512]{2,1,0:T(8,128)S(1)} %select_maximum_fusion.2, ...), kind=kOutput, calls=%fused_computation.8.clone.1 | convolution fusion | flops 1097859072 | bytes 25755648 | tf_op jit(solution)/shard_map/while/body/eval_jaxpr/kgtn,nkd->kgtd/dot_general | solution.py:29
  209.3 2.9 fusion.35
  212.2 4.0 fusion.36
  216.3 8.6 %fusion.38 = f32[2,8,512,128]{3,2,1,0:T(8,128)} fusion(f32[2,8,512,128]{3,2,1,0:T(8,128)} %get-tuple-element.304, f32[2,8,512]{2,1,0:T(8,128)S(1)} %get-tuple-element.286, pred[]{:T(512)S(6)} %compare.23, f32[2,512,8,512]{3,1,2,0:T(8,128)S(1)} %get-tuple-element.284, f32[2,8,512]{2,1,0:T(8,128)S(1)} %select_maximum_fusion.2, ...), kind=kOutput, calls=%fused_computation.8.clone.1 | convolution fusion | flops 1097859072 | bytes 25755648 | tf_op jit(solution)/shard_map/while/body/eval_jaxpr/kgtn,nkd->kgtd/dot_general | solution.py:29
  224.9 5.4 %copy.22 = f32[2,8,512,128]{2,3,1,0:T(8,128)} copy(f32[2,8,512,128]{3,2,1,0:T(8,128)} %get-tuple-element.134) | data formatting | bytes 8388608 | tf_op jit(solution)/shard_map/while | solution.py:65
  233.1 26.0 %convolution_convert_fusion = bf16[512,8192]{1,0:T(8,128)(2,1)} fusion(bf16[512,2048]{0,1:T(8,128)(2,1)S(1)} %bitcast.52, bf16[2048,8192]{1,0:T(8,128)(2,1)} %param.10), kind=kOutput, calls=%fused_computation.35 | convolution fusion | flops 17184063488 | bytes 44040192 | tf_op jit(solution)/shard_map/dot_general | solution.py:71
  259.1 144.4 %reduce-scatter.2.cloned.1.call-done = bf16[512,2048]{1,0:T(8,128)(2,1)} async-done(((bf16[512,8192]{1,0:T(8,128)(2,1)}), bf16[512,2048]{1,0:T(8,128)(2,1)}) %reduce-scatter.2.cloned.1.call-update) | async-done | bytes 2097168 | tf_op jit(solution)/shard_map/reduce_scatter | solution.py:72
  (90 shorter events, 34.6 us)
Async XLA Ops:
  6.5 31.7 %all-gather.3.cloned.1.call-start = ((), (), s32[]{:S(2)}) async-start(), calls=%async_computation.1 | async-start | bytes 2359296 | tf_op jit(solution)/shard_map/all_gather | solution.py:51
  7.3 60.8 %all-gather.5.cloned.1.call-start = ((), (), s32[]{:S(2)}) async-start(), calls=%async_computation.2 | async-start | bytes 2359296 | tf_op jit(solution)/shard_map/all_gather | solution.py:52
  8.0 395.5 %reduce-scatter.2.cloned.1.call-start = ((), (), s32[]{:S(2)}) async-start(), calls=%async_computation.3 | async-start | bytes 10485760 | tf_op jit(solution)/shard_map/reduce_scatter | solution.py:72
  8.1 7.0 %copy-start = (s32[16]{0:T(128)S(1)}, s32[16]{0:T(128)}, u32[]{:S(2)}) copy-start(s32[16]{0:T(128)} %param.11) | copy-start | bytes 196
Sparse Core Ops, SparseCore 0:
  9.2 28.9 all-gather.2
  40.1 27.8 all-gather.4
  259.2 144.2 reduce-scatter.1
where the time goes:
time: 413 us; the launch traced here: 410 us
  waiting for transfers between devices  195 us (47%)
  matrix products  117 us (28%)
  local copies, waits for them, and re-layouts  41.8 us (10%)
  other arithmetic  37.8 us (9%)
  between operations  13.2 us (3%)
  loops' own time  5.01 us (1%)
    reduce_scatter x1, waiting for transfers between devices, per_device(): lax.psum_scatter(partial_out.astype(jnp.bfloat16), 'head', scatter_dimens...  144 us
    dot_general x8, matrix products, attend(): jnp.einsum('kgtn,nkd->kgtd', weight.astype(jnp.bfloat16), v_block, prefer...  68.1 us
    reduce_sum x8, other arithmetic, attend(): total = total * factor + jnp.sum(weight, axis=-1)  32 us
    dot_general x1, matrix products, per_device(): partial_out = jnp.dot(attended, w_out, preferred_element_type=jnp.float32)  26 us
    all_gather x1, waiting for transfers between devices, per_device(): v_piece = lax.all_gather(values, 'blk', axis=0, tiled=True)  25.9 us
    dot_general x8, matrix products, attend(): jnp.einsum('kgtd,nkd->kgtn', q_heads, k_block, preferred_element_type=jnp...  23.3 us
    all_gather x1, waiting for transfers between devices, per_device(): k_piece = lax.all_gather(keys, 'blk', axis=0, tiled=True)  23 us
    dynamic_slice x16, local copies, waits for them, and re-layouts, per_device(): lax.scan(one_block, start_state, (k_blocks, v_blocks, jnp.arange(steps, d...  21.5 us
  transfers between devices with their start and end apart: 3, of which 3 were waited for; matrix products, arithmetic and copies ran while one was open for 3% of the time, Pallas kernels for 0%

commit v1 on v0

v1 whole, which is shorter than its diff:
```python
import functools
import math

import jax
import jax.numpy as jnp
from jax import lax
from jax.experimental import pallas as pl
from jax.experimental.pallas import tpu as pltpu
from jax.sharding import PartitionSpec as P

HD = 128
NT = (((1,), (1,)), ((), ()))


def attend_kernel(half, tile, chunk, order_ref, me_ref, q_ref, k_ref, v_ref, o_ref,
                  inv, q_rows, v_wide, acc, top):
    blocks = order_ref.shape[0]
    tok = q_ref.shape[0]
    group = q_ref.shape[1] // HD
    rows = group * tok
    factor = HD ** (-0.5) * math.log2(math.e)
    start = chunk * tok
    offset = start % half
    own = me_ref[0] + start // half

    def invert(b, _):
        inv[order_ref[b]] = b
        return 0

    lax.fori_loop(0, blocks, invert, 0)
    for g in range(group):
        q_rows[g * tok:(g + 1) * tok, :] = q_ref[:, g * HD:(g + 1) * HD]
    v_wide[:, :HD] = v_ref[...]
    v_wide[:, HD:] = jnp.ones((v_wide.shape[0], HD), v_wide.dtype)
    earlier = order_ref[own]

    def block_of(ref, b):
        return ref[pl.ds(pl.multiple_of(b * half, half), half), :]

    def first(blocks_in):
        k_cat = jnp.concatenate([block_of(k_ref, b) for b in blocks_in], axis=0)
        v_cat = jnp.concatenate([block_of(v_wide, b) for b in blocks_in], axis=0)
        width = k_cat.shape[0]
        query = lax.rem(lax.broadcasted_iota(jnp.int32, (tile, width), 0), tok) + offset
        key = lax.broadcasted_iota(jnp.int32, (tile, width), 1) - (width - half)
        seen = key <= query
        for r in range(0, rows, tile):
            score = lax.dot_general(q_rows[r:r + tile, :], k_cat, NT,
                                    preferred_element_type=jnp.float32)
            score = jnp.where(seen, score, -1e30)
            peak = jnp.max(score, axis=1, keepdims=True)
            weight = jnp.exp2((score - peak) * factor)
            top[r:r + tile, :] = jnp.broadcast_to(peak, (tile, HD))
            acc[r:r + tile, :] = jnp.dot(weight.astype(jnp.bfloat16), v_cat,
                                         preferred_element_type=jnp.float32)

    odd = lax.rem(earlier, 2) == 1

    @pl.when(odd)
    def _():
        first([inv[jnp.maximum(earlier - 1, 0)], own])

    @pl.when(jnp.logical_not(odd))
    def _():
        first([own])

    def step(n, _):
        pair = [inv[2 * n], inv[2 * n + 1]]
        k_cat = jnp.concatenate([block_of(k_ref, b) for b in pair], axis=0)
        v_cat = jnp.concatenate([block_of(v_wide, b) for b in pair], axis=0)
        for r in range(0, rows, tile):
            score = lax.dot_general(q_rows[r:r + tile, :], k_cat, NT,
                                    preferred_element_type=jnp.float32)
            old = top[r:r + tile, :]
            peak = jnp.maximum(old, jnp.max(score, axis=1, keepdims=True))
            top[r:r + tile, :] = peak
            wide = jnp.concatenate([peak] * (2 * half // HD), axis=1)
            weight = jnp.exp2((score - wide) * factor)
            shrink = jnp.exp2((old - peak) * factor)
            acc[r:r + tile, :] = acc[r:r + tile, :] * jnp.concatenate(
                [shrink, shrink], axis=1) + jnp.dot(
                    weight.astype(jnp.bfloat16), v_cat, preferred_element_type=jnp.float32)
        return 0

    lax.fori_loop(0, earlier // 2, step, 0)
    for g in range(group):
        part = acc[g * tok:(g + 1) * tok, :]
        o_ref[:, g * HD:(g + 1) * HD] = (part[:, :HD] / part[:, HD:]).astype(o_ref.dtype)


def attend(queries, k_all, v_all, order, me, chunk, tok, half):
    kv_local = k_all.shape[1] // HD
    width = queries.shape[1] // kv_local
    group = width // HD
    keys = k_all.shape[0]
    rows = group * tok
    tile = min(rows, 256)
    work = rows * keys * kv_local
    return pl.pallas_call(
        functools.partial(attend_kernel, half, tile, chunk),
        out_shape=jax.ShapeDtypeStruct((tok, queries.shape[1]), jnp.bfloat16),
        grid_spec=pltpu.PrefetchScalarGridSpec(
            num_scalar_prefetch=2,
            grid=(kv_local,),
            in_specs=[
                pl.BlockSpec((tok, width), lambda h, *_: (chunk, h)),
                pl.BlockSpec((keys, HD), lambda h, *_: (0, h)),
                pl.BlockSpec((keys, HD), lambda h, *_: (0, h)),
            ],
            out_specs=pl.BlockSpec((tok, width), lambda h, *_: (0, h)),
            scratch_shapes=[
                pltpu.SMEM((order.shape[0],), jnp.int32),
                pltpu.VMEM((rows, HD), jnp.bfloat16),
                pltpu.VMEM((keys, 2 * HD), jnp.bfloat16),
                pltpu.VMEM((rows, 2 * HD), jnp.float32),
                pltpu.VMEM((rows, HD), jnp.float32),
            ],
        ),
        compiler_params=pltpu.CompilerParams(vmem_limit_bytes=40 * 2 ** 20),
        cost_estimate=pl.CostEstimate(
            flops=4 * work * HD, bytes_accessed=4 * keys * HD * kv_local, transcendentals=work),
    )(order, me, queries, k_all, v_all)


def per_device(queries, keys, values, w_out, order):
    tok = queries.shape[0]
    half = tok // 2
    part = tok // 4
    me = (lax.axis_index("blk") * 2).astype(jnp.int32).reshape(1)
    k_all = lax.all_gather(keys, "blk", axis=0, tiled=True)
    v_all = lax.all_gather(values, "blk", axis=0, tiled=True)
    outs = []
    for c in range(tok // part):
        attended = attend(queries, k_all, v_all, order, me, c, part, half)
        share = jnp.dot(attended, w_out, preferred_element_type=jnp.float32).astype(jnp.bfloat16)
        outs.append(lax.psum_scatter(share, "head", scatter_dimension=1, tiled=True))
    return jnp.concatenate(outs, axis=0)


def solution(mesh):
    return jax.shard_map(
        per_device,
        mesh=mesh,
        in_specs=(P("blk", "head"), P("blk", "head"), P("blk", "head"), P("head", None), P()),
        out_specs=P("blk", "head"),
        check_vma=False,
    )
```

time: 413 us -> 300 us (0.73)
  matrix products: 117 us -> 66.6 us
  Pallas kernels: 0 us -> 49 us
  waiting for transfers between devices: 195 us -> 149 us
  other arithmetic: 37.8 us -> 3.08 us
  local copies, waits for them, and re-layouts: 41.8 us -> 15 us
  loops' own time: 5.01 us -> 0 us
    reduce_scatter x1 -> x4, waiting for transfers between devices: 144 us -> 87.2 us  [per_device(): lax.psum_scatter(share, 'head', scatter_dimension=1, tiled=True)]
    dot_general x17 -> x4, matrix products: 117 us -> 66.6 us  [per_device(): jnp.dot(attended, w_out, preferred_element_type=jnp.float32)]
    pallas_call x0 -> x4, Pallas kernels: none -> 49 us  [attend(): pl.pallas_call(functools.partial(attend_kernel, half, tile, chunk), out_s...]
    reduce_sum x17 -> x0, other arithmetic: 32.8 us -> none  [the longest x8 32 us: attend(): total = total * factor + jnp.sum(weight, axis=-1)]
    dynamic_slice x16 -> x0, local copies, waits for them, and re-layouts: 21.5 us -> none  [per_device(): lax.scan(one_block, start_state, (k_blocks, v_blocks, jnp.arange(steps, d...]
    all_gather x2, waiting for transfers between devices: 48.9 us -> 60 us  [the longest x1 30.2 us: per_device(): k_all = lax.all_gather(keys, 'blk', axis=0, tiled=True)]
    unnamed x4 -> x24, local copies, waits for them, and re-layouts: 6.97 us -> 15 us
    reshape x2 -> x0, local copies, waits for them, and re-layouts: 7.93 us -> none  [the longest x1 3.97 us: per_device(): v_blocks = v_piece.reshape(steps, width, kv_local, head_size)]
  transfers between devices with their start and end apart: 3 -> 6, of which waited for: 3 -> 4; matrix products, arithmetic and copies ran while one was open for 3% -> 17% of each run, Pallas kernels for 0% -> 13%
where the time goes in v1:
time: 300 us; the launch traced here: 297 us
  waiting for transfers between devices  149 us (50%)
  matrix products  66.6 us (22%)
  Pallas kernels  49 us (16%)
  local copies, waits for them, and re-layouts  15 us (5%)
  between operations  13.6 us (5%)
  other arithmetic  3.08 us (1%)
    reduce_scatter x4, waiting for transfers between devices, per_device(): lax.psum_scatter(share, 'head', scatter_dimension=1, tiled=True)  87.2 us
    dot_general x4, matrix products, per_device(): jnp.dot(attended, w_out, preferred_element_type=jnp.float32)  66.6 us
    pallas_call x4, Pallas kernels, attend(): pl.pallas_call(functools.partial(attend_kernel, half, tile, chunk), out_s...  49 us
    all_gather x1, waiting for transfers between devices, per_device(): k_all = lax.all_gather(keys, 'blk', axis=0, tiled=True)  30.2 us
    all_gather x1, waiting for transfers between devices, per_device(): v_all = lax.all_gather(values, 'blk', axis=0, tiled=True)  29.8 us
    unnamed x24, local copies, waits for them, and re-layouts  15 us
  transfers between devices with their start and end apart: 6, of which 4 were waited for; matrix products, arithmetic and copies ran while one was open for 17% of the time, Pallas kernels for 13%

profile of v1, /device:TPU:12, one launch (start us, length us, event | category | flops | bytes accessed | tf_op | source)
XLA Modules:
  0.0 296.8 jit_solution(8119403540503639345)
XLA Ops:
  6.5 0.7 all-gather.3.cloned.1.call-update
  7.3 0.0 all-gather.5.cloned.1.call-start
  7.3 0.7 all-gather.5.cloned.1.call-update
  8.0 0.0 reduce-scatter.5.cloned.1.call-start
  8.1 30.2 %all-gather.3.cloned.1.call-done.k_ref = bf16[4096,256]{1,0:T(8,128)(2,1)} async-done(((bf16[512,256]{1,0:T(8,128)(2,1)}), bf16[4096,256]{1,0:T(8,128)(2,1)}) %all-gather.3.cloned.1.call-update) | async-done | bytes 2097168 | tf_op jit(solution)/shard_map/all_gather | solution.py:130
  38.2 29.8 %all-gather.5.cloned.1.call-done.v_ref = bf16[4096,256]{1,0:T(8,128)(2,1)} async-done(((bf16[512,256]{1,0:T(8,128)(2,1)}), bf16[4096,256]{1,0:T(8,128)(2,1)}) %all-gather.5.cloned.1.call-update) | async-done | bytes 2097168 | tf_op jit(solution)/shard_map/all_gather | solution.py:131
  68.0 1.6 copy-done
  69.6 1.6 copy-done.2
  71.2 1.6 copy-done.6
  72.8 0.7 copy-done.10
  73.5 9.9 %shard_map.55 = bf16[128,2048]{1,0:T(8,128)(2,1)S(1)} custom-call(s32[16]{0:T(128)S(1)} %copy-done.10, s32[1]{0:T(128)} %bitcast.me_ref, bf16[512,2048]{1,0:T(8,128)(2,1)S(1)} %copy-done, bf16[4096,256]{1,0:T(8,128)(2,1)S(1)} %copy-done.2, bf16[4096,256]{1,0:T(8,128)(2,1)S(1)} %copy-done.6), custom_call_target="tpu_custom_call" | custom-call | flops 4294967296 | bytes 4194304 | tf_op jit(solution)/shard_map/pallas_call | solution.py:99
  83.4 16.6 %convolution_convert_fusion.3 = bf16[128,8192]{1,0:T(8,128)(2,1)} fusion(bf16[128,2048]{1,0:T(8,128)(2,1)S(1)} %shard_map.55, bf16[2048,8192]{1,0:T(8,128)(2,1)} %param.8), kind=kOutput, calls=%fused_computation.3 | convolution fusion | flops 4296015872 | bytes 36175872 | tf_op jit(solution)/shard_map/dot_general | solution.py:135
  100.0 0.2 reduce-scatter.7.cloned.1.call-start
  100.2 1.6 copy-done.3
  101.8 1.6 copy-done.7
  103.4 9.9 %shard_map.56 = bf16[128,2048]{1,0:T(8,128)(2,1)S(1)} custom-call(s32[16]{0:T(128)S(1)} %copy-done.11, s32[1]{0:T(128)} %bitcast.me_ref, bf16[512,2048]{1,0:T(8,128)(2,1)S(1)} %copy-done.1, bf16[4096,256]{1,0:T(8,128)(2,1)S(1)} %copy-done.3, bf16[4096,256]{1,0:T(8,128)(2,1)S(1)} %copy-done.7), custom_call_target="tpu_custom_call" | custom-call | flops 4294967296 | bytes 4194304 | tf_op jit(solution)/shard_map/pallas_call | solution.py:99
  113.3 16.9 %convolution_convert_fusion.2 = bf16[128,8192]{1,0:T(8,128)(2,1)} fusion(bf16[128,2048]{1,0:T(8,128)(2,1)S(1)} %shard_map.56, bf16[2048,8192]{1,0:T(8,128)(2,1)} %param.8), kind=kOutput, calls=%fused_computation.2 | convolution fusion | flops 4296015872 | bytes 36175872 | tf_op jit(solution)/shard_map/dot_general | solution.py:135
  130.2 0.3 reduce-scatter.9.cloned.1.call-start
  130.5 1.6 copy-done.4
  132.1 1.6 copy-done.8
  133.7 14.6 %shard_map.57 = bf16[128,2048]{1,0:T(8,128)(2,1)S(1)} custom-call(s32[16]{0:T(128)S(1)} %copy-done.11, s32[1]{0:T(128)} %bitcast.me_ref, bf16[512,2048]{1,0:T(8,128)(2,1)S(1)} %copy-done.1, bf16[4096,256]{1,0:T(8,128)(2,1)S(1)} %copy-done.4, bf16[4096,256]{1,0:T(8,128)(2,1)S(1)} %copy-done.8), custom_call_target="tpu_custom_call" | custom-call | flops 4294967296 | bytes 4194304 | tf_op jit(solution)/shard_map/pallas_call | solution.py:99
  148.3 16.6 %convolution_convert_fusion.1 = bf16[128,8192]{1,0:T(8,128)(2,1)} fusion(bf16[128,2048]{1,0:T(8,128)(2,1)S(1)} %shard_map.57, bf16[2048,8192]{1,0:T(8,128)(2,1)} %param.8), kind=kOutput, calls=%fused_computation.1 | convolution fusion | flops 4296015872 | bytes 36175872 | tf_op jit(solution)/shard_map/dot_general | solution.py:135
  164.9 0.3 reduce-scatter.11.cloned.1.call-start
  165.2 1.6 copy-done.5
  166.8 1.6 copy-done.9
  168.4 14.6 %shard_map.58 = bf16[128,2048]{1,0:T(8,128)(2,1)S(1)} custom-call(s32[16]{0:T(128)S(1)} %copy-done.11, s32[1]{0:T(128)} %bitcast.me_ref, bf16[512,2048]{1,0:T(8,128)(2,1)S(1)} %copy-done.1, bf16[4096,256]{1,0:T(8,128)(2,1)S(1)} %copy-done.5, bf16[4096,256]{1,0:T(8,128)(2,1)S(1)} %copy-done.9), custom_call_target="tpu_custom_call" | custom-call | flops 4294967296 | bytes 4194304 | tf_op jit(solution)/shard_map/pallas_call | solution.py:99
  183.0 16.5 %convolution_convert_fusion = bf16[128,8192]{1,0:T(8,128)(2,1)} fusion(bf16[128,2048]{1,0:T(8,128)(2,1)S(1)} %shard_map.58, bf16[2048,8192]{1,0:T(8,128)(2,1)} %param.8), kind=kOutput, calls=%fused_computation | convolution fusion | flops 4296015872 | bytes 36175872 | tf_op jit(solution)/shard_map/dot_general | solution.py:135
  199.6 0.0 reduce-scatter.5.cloned.1.call-done
  199.6 0.0 reduce-scatter.7.cloned.1.call-done
  199.6 41.7 %reduce-scatter.9.cloned.1.call-done = bf16[128,2048]{1,0:T(8,128)(2,1)} async-done(((bf16[128,8192]{1,0:T(8,128)(2,1)}), bf16[128,2048]{1,0:T(8,128)(2,1)}) %reduce-scatter.9.cloned.1.call-update) | async-done | bytes 524304 | tf_op jit(solution)/shard_map/reduce_scatter | solution.py:136
  241.4 45.5 %reduce-scatter.11.cloned.1.call-done = bf16[128,2048]{1,0:T(8,128)(2,1)} async-done(((bf16[128,8192]{1,0:T(8,128)(2,1)}), bf16[128,2048]{1,0:T(8,128)(2,1)}) %reduce-scatter.11.cloned.1.call-update) | async-done | bytes 524304 | tf_op jit(solution)/shard_map/reduce_scatter | solution.py:136
  286.8 3.1 %pad_maximum_fusion = bf16[512,2048]{1,0:T(8,128)(2,1)} fusion(bf16[128,2048]{1,0:T(8,128)(2,1)} %reduce-scatter.11.cloned.1.call-done, bf16[128,2048]{1,0:T(8,128)(2,1)} %reduce-scatter.9.cloned.1.call-done, bf16[128,2048]{1,0:T(8,128)(2,1)} %reduce-scatter.7.cloned.1.call-done, bf16[128,2048]{1,0:T(8,128)(2,1)} %reduce-scatter.5.cloned.1.call-done), kind=kLoop, calls=%fused_computation.4 | loop fusion | flops 8388608 | bytes 4194304 | tf_op jit(solution)/shard_map/concatenate | solution.py:137
  (19 shorter events, 0.1 us)
Async XLA Ops:
  6.5 31.7 %all-gather.3.cloned.1.call-start = ((), (), s32[]{:S(2)}) async-start(), calls=%async_computation.4 | async-start | bytes 2359296 | tf_op jit(solution)/shard_map/all_gather | solution.py:130
  7.3 60.8 %all-gather.5.cloned.1.call-start = ((), (), s32[]{:S(2)}) async-start(), calls=%async_computation.5 | async-start | bytes 2359296 | tf_op jit(solution)/shard_map/all_gather | solution.py:131
  8.0 191.6 %reduce-scatter.5.cloned.1.call-start = ((), (), s32[]{:S(2)}) async-start(), calls=%async_computation.6 | async-start | bytes 2621440 | tf_op jit(solution)/shard_map/reduce_scatter | solution.py:136
  68.0 1.6 copy-start
  69.6 1.6 copy-start.2
  71.2 1.6 copy-start.6
  72.8 0.7 copy-start.10
  83.3 16.9 %copy-start.1 = (bf16[512,2048]{1,0:T(8,128)(2,1)S(1)}, bf16[512,2048]{1,0:T(8,128)(2,1)}, u32[]{:S(2)}) copy-start(bf16[512,2048]{1,0:T(8,128)(2,1)} %q_ref.7) | copy-start | bytes 6291460
  83.4 16.9 %copy-start.11 = (s32[16]{0:T(128)S(1)}, s32[16]{0:T(128)}, u32[]{:S(2)}) copy-start(s32[16]{0:T(128)} %order_ref.7) | copy-start | bytes 196
  100.0 99.6 %reduce-scatter.7.cloned.1.call-start = ((), (), s32[]{:S(2)}) async-start(), calls=%async_computation.7 | async-start | bytes 2621440 | tf_op jit(solution)/shard_map/reduce_scatter | solution.py:136
  100.2 1.6 copy-start.3
  101.8 1.6 copy-start.7
  130.2 111.2 %reduce-scatter.9.cloned.1.call-start = ((), (), s32[]{:S(2)}) async-start(), calls=%async_computation.8 | async-start | bytes 2621440 | tf_op jit(solution)/shard_map/reduce_scatter | solution.py:136
  130.5 1.6 copy-start.4
  132.1 1.6 copy-start.8
  164.9 121.9 %reduce-scatter.11.cloned.1.call-start = ((), (), s32[]{:S(2)}) async-start(), calls=%async_computation.9 | async-start | bytes 2621440 | tf_op jit(solution)/shard_map/reduce_scatter | solution.py:136
  165.2 1.6 copy-start.5
  166.8 1.6 copy-start.9
Sparse Core Ops, SparseCore 0:
  9.2 28.9 all-gather.2
  40.1 27.8 all-gather.4
  100.1 50.4 reduce-scatter.4
  152.8 43.1 reduce-scatter.6
  198.2 43.1 reduce-scatter.8
  243.6 43.1 reduce-scatter.10
